TPU v7x, 32 devices: a whole 2x2x4 slice. The times are simulated.
32 devices in a mesh: section: 2 (over x), wide: 16 (over z, y, core).
Axes of the slice: x: 2, y: 2, z: 4, core: 2. Of those that a mesh axis runs over, the one named last changes fastest.
Arguments:
- features: float32 [2, 5120, 512], P(None, 'wide'), may hold values from -6 to 6
- sigma_embed: bfloat16 [2, 512], replicated, may hold values from -6 to 6
- cotangent: float32 [2, 5120, 512], P(None, 'wide'), may hold values from -6 to 6
- neighbours: int32 [5120, 16], P('wide'), may hold values from 0 to 5119, as said below
- valid_slots: int32 [5120, 16], P('wide'), may hold values from 0 to 1, as said below
- ada_weight: bfloat16 [2, 512, 2048], P('section'), may hold values from -0.0625 to 0.0625
- ada_bias: float32 [2, 2048], P('section'), may hold values from -4 to 4
- qkv_weight: bfloat16 [2, 512, 1536], P('section'), may hold values from -0.25 to 0.25
- out_weight: bfloat16 [2, 512, 512], P('section'), may hold values from -1 to 1
- up_weight: bfloat16 [2, 512, 2048], P('section'), may hold values from -0.25 to 0.25
- up_bias: float32 [2, 2048], P('section'), may hold values from -6 to 6
- down_weight: bfloat16 [2, 2048, 512], P('section'), may hold values from -0.125 to 0.125
- down_bias: float32 [2, 512], P('section'), may hold values from -4 to 4
Outputs:
- boundary: float32 [2, 2, 5120, 512], P('section', None, 'wide')
- grad_ada_weight: float32 [2, 512, 2048], P('section')
- grad_ada_bias: float32 [2, 2048], P('section')
- grad_qkv_weight: float32 [2, 512, 1536], P('section')
- grad_out_weight: float32 [2, 512, 512], P('section')
- grad_up_weight: float32 [2, 512, 2048], P('section')
- grad_up_bias: float32 [2, 2048], P('section')
- grad_down_weight: float32 [2, 2048, 512], P('section')
- grad_down_bias: float32 [2, 512], P('section')
Inputs may be any that keep to these rules, and one draw needn't show every extreme that they name: `neighbours`: node numbers of one micro-batch's mesh; column 0 is the node itself; every entry lies within 320 places of its node, counted cyclically over 5120, and that distance is met in both directions. `valid_slots`: column 0 is always 1.
All inputs are finite; a program needn't handle non-finite values.
Results may differ from a plain program's by a relative error of at most 0.015.
Values may be sent and summed in bfloat16 or wider, within the bound.
A program may use at most 192 MiB of HBM per device.

v0:
```python
import jax
import jax.numpy as jnp
from jax import lax
from jax.sharding import PartitionSpec as P

D = 512
FF = 2048
HEADS = 4
HEAD_DIM = 128
NEIGHBOURS = 16
MICRO = 2


norm_epsilon = 1e-05
masked_score = -1e30


def with_halo(cells, sides, width):
    for axis, dim in sides:
        count = lax.axis_size(axis)
        head = lax.slice_in_dim(cells, 0, width, axis=dim)
        tail = lax.slice_in_dim(cells, cells.shape[dim] - width, cells.shape[dim], axis=dim)
        cells = jnp.concatenate(
            [
                lax.ppermute(tail, axis, [(i, (i + 1) % count) for i in range(count)]),
                cells,
                lax.ppermute(head, axis, [((i + 1) % count, i) for i in range(count)]),
            ],
            axis=dim,
        )
    return cells


def shifted(value, axis, steps):
    count = lax.axis_size(axis)
    first, last = (max(0, -steps), min(count, count - steps))
    return lax.ppermute(value, axis, [(source, source + steps) for source in range(first, last)])


def normalize(values):
    center = values - jnp.mean(values, axis=-1, keepdims=True)
    spread = jnp.mean(center * center, axis=-1, keepdims=True)
    return center * lax.rsqrt(spread + norm_epsilon)


def modulate(values, shift, scale):
    return normalize(values) * (1.0 + scale) + shift


def swish(values):
    return values * jax.nn.sigmoid(values)


def rows_product(left, right):
    return lax.dot_general(
        left, right, (((0,), (0,)), ((), ())), preferred_element_type=jnp.float32
    )


def cross_product(left, right):
    return lax.dot_general(
        left, right, (((1,), (1,)), ((), ())), preferred_element_type=jnp.float32
    )


def split_heads(packed):
    return packed.reshape(packed.shape[:-1] + (HEADS, HEAD_DIM))


def make_modulation(weights, embed_row):
    return (
        jnp.dot(embed_row[None, :], weights[0], preferred_element_type=jnp.float32)[0] + weights[1]
    )


def widen_rim(key_value):
    return with_halo(key_value, (("wide", 0),), key_value.shape[0])


def pre_attention(layer_in, modulation, weights):
    normed_a = modulate(layer_in, modulation[:D], modulation[D : 2 * D]).astype(jnp.bfloat16)
    mixed_qkv = jnp.dot(normed_a, weights[2], preferred_element_type=jnp.float32).astype(
        jnp.bfloat16
    )
    return (normed_a, mixed_qkv, widen_rim(mixed_qkv[:, D:]))


def head_scores(queries, near_rows, valid_slots):
    scores = jnp.einsum(
        "nhe,nkhe->nkh",
        split_heads(queries),
        split_heads(near_rows[:, :, :D]),
        preferred_element_type=jnp.float32,
    ) * HEAD_DIM ** (-0.5)
    return jnp.where(valid_slots[:, :, None] > 0, scores, masked_score)


def attention_forward(queries, near_rows, valid_slots):
    row_count = queries.shape[0]
    scores = head_scores(queries, near_rows, valid_slots)
    row_top = jnp.max(scores, axis=1, keepdims=True)
    raised = jnp.exp(scores - row_top)
    total_weight = jnp.sum(raised, axis=1, keepdims=True)
    soft_weights = raised / total_weight
    attended = jnp.einsum(
        "nkh,nkhe->nhe",
        soft_weights,
        split_heads(near_rows[:, :, D:]),
        precision=lax.Precision.HIGHEST,
        preferred_element_type=jnp.float32,
    )
    return (attended.reshape(row_count, D), row_top + jnp.log(total_weight))


def attention_backward(queries, near_rows, valid_slots, log_total, grad_attended):
    row_count = queries.shape[0]
    soft_weights = jnp.exp(head_scores(queries, near_rows, valid_slots) - log_total)
    key_heads = split_heads(near_rows[:, :, :D])
    value_heads = split_heads(near_rows[:, :, D:])
    query_heads = split_heads(queries).astype(jnp.float32)
    grad_heads = split_heads(grad_attended)
    grad_soft = jnp.einsum(
        "nhe,nkhe->nkh",
        grad_heads,
        value_heads,
        precision=lax.Precision.HIGHEST,
        preferred_element_type=jnp.float32,
    )
    grad_values = soft_weights[:, :, :, None] * grad_heads[:, None, :, :]
    grad_scores = (
        soft_weights
        * (grad_soft - jnp.sum(soft_weights * grad_soft, axis=1, keepdims=True))
        * HEAD_DIM ** (-0.5)
    )
    grad_queries = jnp.einsum(
        "nkh,nkhe->nhe",
        grad_scores,
        key_heads,
        precision=lax.Precision.HIGHEST,
        preferred_element_type=jnp.float32,
    )
    grad_keys = grad_scores[:, :, :, None] * query_heads[:, None, :, :]
    grad_near = jnp.concatenate(
        [
            grad_keys.reshape(row_count, NEIGHBOURS, D),
            grad_values.reshape(row_count, NEIGHBOURS, D),
        ],
        axis=2,
    )
    return (grad_queries.reshape(row_count, D), grad_near)


def layer_tail(layer_in, modulation, weights, mixed_qkv, key_rim, places, valid_slots):
    near_rows = key_rim[places]
    attended, log_total = attention_forward(mixed_qkv[:, :D], near_rows, valid_slots)
    attended_low = attended.astype(jnp.bfloat16)
    mixed = layer_in + jnp.dot(attended_low, weights[3], preferred_element_type=jnp.float32)
    normed_b = modulate(mixed, modulation[2 * D : 3 * D], modulation[3 * D :]).astype(jnp.bfloat16)
    hidden = jnp.dot(normed_b, weights[4], preferred_element_type=jnp.float32) + weights[5]
    active = swish(hidden).astype(jnp.bfloat16)
    output = mixed + jnp.dot(active, weights[6], preferred_element_type=jnp.float32) + weights[7]
    return (output, (attended_low, log_total, mixed, normed_b, hidden, active))


def layer_backward(
    layer_in, modulation, weights, rim_parts, tail_parts, places, valid_slots, grad_out
):
    normed_a, mixed_qkv, key_rim = rim_parts
    attended_low, log_total, mixed, normed_b, hidden, active = tail_parts
    row_count = layer_in.shape[0]
    near_rows = key_rim[places]
    grad_low = grad_out.astype(jnp.bfloat16)
    grad_down = rows_product(active, grad_low)
    grad_down_bias = jnp.sum(grad_out, axis=0)
    grad_active = cross_product(grad_low, weights[6])
    swish_value, swish_back = jax.vjp(swish, hidden)
    grad_hidden = swish_back(grad_active)[0].astype(jnp.bfloat16)
    grad_up_bias = jnp.sum(grad_hidden.astype(jnp.float32), axis=0)
    grad_up = rows_product(normed_b, grad_hidden)
    grad_normed_b = cross_product(grad_hidden, weights[4])
    norm_value, norm_back = jax.vjp(modulate, mixed, modulation[2 * D : 3 * D], modulation[3 * D :])
    grad_mixed_part, grad_shift_b, grad_scale_b = norm_back(grad_normed_b)
    grad_mixed = grad_out + grad_mixed_part
    grad_mixed_low = grad_mixed.astype(jnp.bfloat16)
    grad_out_weight = rows_product(attended_low, grad_mixed_low)
    grad_attended = cross_product(grad_mixed_low, weights[3])
    grad_queries, grad_near = attention_backward(
        mixed_qkv[:, :D], near_rows, valid_slots, log_total, grad_attended
    )
    grad_rim = jax.ops.segment_sum(
        grad_near.reshape(row_count * NEIGHBOURS, 2 * D),
        places.reshape(-1),
        num_segments=3 * row_count,
    )
    outer_rows = jnp.concatenate([grad_rim[:row_count], grad_rim[2 * row_count :]], axis=0)
    returned = with_halo(outer_rows.astype(jnp.bfloat16), (("wide", 0),), row_count).astype(
        outer_rows.dtype
    )
    grad_key_value = (
        grad_rim[row_count : 2 * row_count] + returned[:row_count] + returned[3 * row_count :]
    )
    grad_qkv = jnp.concatenate([grad_queries, grad_key_value], axis=1).astype(jnp.bfloat16)
    grad_qkv_weight = rows_product(normed_a, grad_qkv)
    grad_normed_a = cross_product(grad_qkv, weights[2])
    norm_value_a, norm_back_a = jax.vjp(modulate, layer_in, modulation[:D], modulation[D : 2 * D])
    grad_in_part, grad_shift_a, grad_scale_a = norm_back_a(grad_normed_a)
    grad_in = grad_mixed + grad_in_part
    grad_mod = jnp.concatenate([grad_shift_a, grad_scale_a, grad_shift_b, grad_scale_b])
    return (
        grad_in,
        grad_mod,
        (grad_qkv_weight, grad_out_weight, grad_up, grad_up_bias, grad_down, grad_down_bias),
    )


def recall(stored, position, empty):
    if 0 <= position < len(stored):
        return stored[position]
    return empty


def shards(
    features,
    sigma_embed,
    cotangent,
    neighbours,
    valid_slots,
    ada_weight,
    ada_bias,
    qkv_weight,
    out_weight,
    up_weight,
    up_bias,
    down_weight,
    down_bias,
):
    weights = (
        ada_weight[0],
        ada_bias[0],
        qkv_weight[0],
        out_weight[0],
        up_weight[0],
        up_bias[0],
        down_weight[0],
        down_bias[0],
    )
    row_count = features.shape[1]
    section_index = lax.axis_index("section")
    first_section = section_index == 0
    places = jnp.remainder(
        neighbours - (lax.axis_index("wide") - 1) * row_count, row_count * lax.axis_size("wide")
    )
    blank = jnp.zeros((row_count, D), jnp.float32)
    blank_tail = (
        jnp.zeros((row_count, D), jnp.bfloat16),
        jnp.zeros((row_count, 1, HEADS), jnp.float32),
        jnp.zeros((row_count, D), jnp.float32),
        jnp.zeros((row_count, D), jnp.bfloat16),
        jnp.zeros((row_count, FF), jnp.float32),
        jnp.zeros((row_count, FF), jnp.bfloat16),
    )
    inputs_kept = []
    tails_kept = []
    outputs = []
    input_grads = [blank]
    arriving = jnp.zeros((row_count, D), jnp.bfloat16)
    returning = jnp.zeros((row_count, D), jnp.bfloat16)
    layer_sums = tuple((jnp.zeros(member.shape, jnp.float32) for member in weights[2:]))
    ada_outer = jnp.zeros(weights[0].shape, jnp.float32)
    ada_bias_sum = jnp.zeros((4 * D,), jnp.float32)

    def pick_embed(position):
        return sigma_embed[jnp.clip(position, 0, MICRO - 1)]

    for moment in range(MICRO + 2):
        if moment <= MICRO:
            fresh_rows = features[moment] if moment < MICRO else blank
            layer_in = jnp.where(first_section, fresh_rows, arriving.astype(jnp.float32))
            modulation = make_modulation(weights, pick_embed(moment - section_index))
            rim_parts = pre_attention(layer_in, modulation, weights)
            output, tail_parts = layer_tail(
                layer_in, modulation, weights, rim_parts[1], rim_parts[2], places, valid_slots
            )
            inputs_kept.append(layer_in)
            tails_kept.append(tail_parts)
            outputs.append(output)
            if moment < MICRO:
                arriving = shifted(output.astype(jnp.bfloat16), "section", 1)
        if moment >= 1:
            position = moment - 2 + section_index
            layer_in = jnp.where(
                first_section,
                recall(inputs_kept, moment - 2, blank),
                recall(inputs_kept, moment, blank),
            )
            embed_row = pick_embed(position)
            modulation = make_modulation(weights, embed_row)
            rim_parts = pre_attention(layer_in, modulation, weights)
            lower_tail = recall(tails_kept, moment - 2, blank_tail)
            upper_tail = recall(tails_kept, moment, blank_tail)
            tail_parts = tuple(
                (
                    jnp.where(first_section, below, above)
                    for below, above in zip(lower_tail, upper_tail)
                )
            )
            sent_down = cotangent[moment - 1] if moment <= MICRO else blank
            grad_out = jnp.where(first_section, returning.astype(jnp.float32), sent_down)
            grad_in, grad_mod, layer_grads = layer_backward(
                layer_in, modulation, weights, rim_parts, tail_parts, places, valid_slots, grad_out
            )
            input_grads.append(grad_in)
            if moment <= MICRO:
                returning = shifted(grad_in.astype(jnp.bfloat16), "section", -1)
            layer_sums = tuple(
                (running + addend for running, addend in zip(layer_sums, layer_grads))
            )
            ada_outer = ada_outer + embed_row.astype(jnp.float32)[:, None] * grad_mod[None, :]
            ada_bias_sum = ada_bias_sum + grad_mod
    boundary = jnp.stack(
        [
            jnp.where(first_section, input_grads[position + 2], outputs[position + 1])
            for position in range(MICRO)
        ]
    )
    summed = lax.psum(
        (
            ada_outer,
            ada_bias_sum,
            layer_sums[0],
            layer_sums[1],
            layer_sums[2],
            layer_sums[3],
            layer_sums[4],
            layer_sums[5],
        ),
        "wide",
    )
    grad_ada_weight = summed[0]
    grad_ada_bias = summed[1]
    remaining = summed[2:]
    return (
        boundary[None],
        grad_ada_weight[None],
        grad_ada_bias[None],
        remaining[0][None],
        remaining[1][None],
        remaining[2][None],
        remaining[3][None],
        remaining[4][None],
        remaining[5][None],
    )


def solution(mesh):
    return jax.shard_map(
        shards,
        mesh=mesh,
        in_specs=(
            P(None, "wide", None),
            P(),
            P(None, "wide", None),
            P("wide", None),
            P("wide", None),
            P("section", None, None),
            P("section", None),
            P("section", None, None),
            P("section", None, None),
            P("section", None, None),
            P("section", None),
            P("section", None, None),
            P("section", None),
        ),
        out_specs=(
            P("section", None, "wide", None),
            P("section", None, None),
            P("section", None),
            P("section", None, None),
            P("section", None, None),
            P("section", None, None),
            P("section", None),
            P("section", None, None),
            P("section", None),
        ),
        check_vma=False,
    )
```

profile of v0, /device:TPU:0, one launch (start us, length us, event | category | flops | bytes accessed | tf_op | source)
XLA Modules:
  0.0 1219.7 jit_solution(9464340149660911150)
XLA Ops:
  32.5 5.8 collective-permute-done
  41.0 27.7 %gather_fusion = bf16[5120,1024]{1,0:T(8,128)(2,1)} fusion(bf16[960,1024]{1,0:T(8,128)(2,1)} %pad_maximum_fusion, s32[5120]{0:T(1024)S(1)} %broadcast_clamp_fusion), kind=kCustom, calls=%fused_computation | custom fusion | bytes 20992000 | tf_op jit(solution)/shard_map/gather | solution.py:154
  68.7 10.5 slice_bitcast_fusion.10
  79.2 5.4 fusion.51
  86.5 6.5 fusion.48
  136.0 27.7 %gather_fusion.1 = bf16[5120,1024]{1,0:T(8,128)(2,1)} fusion(bf16[960,1024]{1,0:T(8,128)(2,1)} %pad_maximum_fusion.1, s32[5120]{0:T(1024)S(1)} %broadcast_clamp_fusion), kind=kCustom, calls=%fused_computation.1 | custom fusion | bytes 20992000 | tf_op jit(solution)/shard_map/gather | solution.py:154
  163.7 10.5 slice_bitcast_fusion.8
  174.2 6.3 fusion.45
  183.5 6.8 fusion.42
  219.0 27.9 %gather_fusion.2 = bf16[5120,1024]{1,0:T(8,128)(2,1)} fusion(bf16[960,1024]{1,0:T(8,128)(2,1)} %pad_maximum_fusion.2, s32[5120]{0:T(1024)S(1)} %broadcast_clamp_fusion), kind=kCustom, calls=%fused_computation.2 | custom fusion | bytes 20992000 | tf_op jit(solution)/shard_map/gather | solution.py:171
  246.9 10.5 slice_bitcast_fusion.6
  257.4 11.0 fusion.35
  282.3 5.6 collective-permute-start.11
  303.2 27.7 %gather_fusion.3 = bf16[5120,1024]{1,0:T(8,128)(2,1)} fusion(bf16[960,1024]{1,0:T(8,128)(2,1)} %pad_maximum_fusion.3, s32[5120]{0:T(1024)S(1)} %broadcast_clamp_fusion), kind=kCustom, calls=%fused_computation.3 | custom fusion | bytes 20992000 | tf_op jit(solution)/shard_map/gather | solution.py:154
  330.9 10.6 slice_bitcast_fusion.4
  348.2 6.4 fusion.29
  362.1 28.1 %gather_fusion.4 = bf16[5120,1024]{1,0:T(8,128)(2,1)} fusion(bf16[960,1024]{1,0:T(8,128)(2,1)} %pad_maximum_fusion.4, s32[5120]{0:T(1024)S(1)} %broadcast_clamp_fusion), kind=kCustom, calls=%fused_computation.4 | custom fusion | bytes 20992000 | tf_op jit(solution)/shard_map/gather | solution.py:171
  390.2 10.6 slice_bitcast_fusion.2
  400.8 6.3 fusion.27
  421.6 6.5 fusion.38
  429.0 7.1 mul.734
  436.1 9.6 bitcast_multiply_fusion.4
  445.7 7.2 mul.729
  452.9 9.3 bitcast_multiply_fusion.5
  462.3 45.8 %scatter_custom_fusion = f32[960,1024]{1,0:T(8,128)} fusion(s32[5120]{0:T(1024)} %reshape.662, f32[5120,512]{1,0:T(8,128)} %bitcast_multiply_fusion.4, f32[]{:T(128)} %constant.98.clone.1, f32[5120,512]{1,0:T(8,128)} %bitcast_multiply_fusion.5, f32[]{:T(128)} %constant.86.clone.1), kind=kCustom, calls=%fused_computation.12 | custom fusion | flops 10485760 | bytes 24904704 | tf_op jit(solution)/shard_map/scatter-add | solution.py:190
  511.6 10.8 collective-permute-start.7
  536.6 7.7 collective-permute-start.18
  566.9 10.8 fusion.22
  583.2 6.9 fusion.25
  591.0 7.1 mul.784
  598.1 9.6 bitcast_multiply_fusion.2
  607.7 7.1 mul.779
  614.8 9.3 bitcast_multiply_fusion.3
  624.0 45.8 %scatter_custom_fusion.1 = f32[960,1024]{1,0:T(8,128)} fusion(s32[5120]{0:T(1024)} %reshape.662, f32[5120,512]{1,0:T(8,128)} %bitcast_multiply_fusion.2, f32[]{:T(128)} %constant.98.clone.1, f32[5120,512]{1,0:T(8,128)} %bitcast_multiply_fusion.3, f32[]{:T(128)} %constant.86.clone.1), kind=kCustom, calls=%fused_computation.16 | custom fusion | flops 10485760 | bytes 24904704 | tf_op jit(solution)/shard_map/scatter-add | solution.py:190
  691.5 27.7 %gather_fusion.5 = bf16[5120,1024]{1,0:T(8,128)(2,1)} fusion(bf16[960,1024]{1,0:T(8,128)(2,1)} %pad_maximum_fusion.5, s32[5120]{0:T(1024)S(1)} %broadcast_clamp_fusion), kind=kCustom, calls=%fused_computation.5 | custom fusion | bytes 20992000 | tf_op jit(solution)/shard_map/gather | solution.py:171
  719.2 10.5 slice_bitcast_fusion
  729.7 5.4 fusion.20
  749.6 6.6 collective-permute-done.17
  763.2 10.8 fusion.15
  782.5 7.2 fusion.18
  789.7 7.1 mul.822
  796.8 9.6 bitcast_multiply_fusion
  806.4 7.1 mul.817
  813.4 9.3 bitcast_multiply_fusion.1
  822.7 46.0 %scatter_custom_fusion.2 = f32[960,1024]{1,0:T(8,128)} fusion(s32[5120]{0:T(1024)} %reshape.662, f32[5120,512]{1,0:T(8,128)} %bitcast_multiply_fusion, f32[]{:T(128)} %constant.98.clone.1, f32[5120,512]{1,0:T(8,128)} %bitcast_multiply_fusion.1, f32[]{:T(128)} %constant.86.clone.1), kind=kCustom, calls=%fused_computation.20 | custom fusion | flops 10485760 | bytes 24904704 | tf_op jit(solution)/shard_map/scatter-add | solution.py:190
  875.9 5.9 add_bitcast_fusion
  899.4 61.7 %all-reduce = (f32[1,2048]{1,0:T(1,128)}, f32[1,2048]{1,0:T(1,128)}, f32[1,512]{1,0:T(1,128)}) all-reduce(f32[1,2048]{1,0:T(1,128)S(1)} %bitcast.571, f32[1,2048]{1,0:T(1,128)S(1)} %bitcast.572, f32[1,512]{1,0:T(1,128)S(1)} %bitcast.573), channel_id=1, replica_groups=mesh['section'=2,'wide'=16] {'wide'}, use_global_device_ids=true, to_apply=%region_61.62 | all-reduce | flops 4608 | bytes 36864 | tf_op jit(solution)/shard_map/psum | solution.py:326
  966.8 231.2 %all-reduce.4.cloned.1.call-done = (f32[1,512,2048]{2,1,0:T(8,128)}, f32[1,512,1536]{2,1,0:T(8,128)}, f32[1,512,512]{2,1,0:T(8,128)}, f32[1,512,2048]{2,1,0:T(8,128)}, f32[1,2048,512]{2,1,0:T(8,128)}) async-done(((f32[1,512,2048]{2,1,0:T(8,128)}, f32[1,512,1536]{2,1,0:T(8,128)}, f32[1,512,512]{2,1,0:T(8,128)}, f32[1,512,2048]{2,1,0:T(8,128)}, f32[1,2048,512]{2,1,0:T(8,128)}), (f32[1,512,2048]{2,1,0:T(8,128)}, ...) | async-done | bytes 16777232 | tf_op jit(solution)/shard_map/psum | solution.py:326
  (641 shorter events, 304.6 us)
Async XLA Ops:
  7.2 88.9 %copy-start = (bf16[1,2048,512]{2,1,0:T(8,128)(2,1)S(1)}, bf16[1,2048,512]{2,1,0:T(8,128)(2,1)}, u32[]{:S(2)}) copy-start(bf16[1,2048,512]{2,1,0:T(8,128)(2,1)} %param.24) | copy-start | bytes 6291460
  7.2 1190.8 %all-reduce.4.cloned.1.call-start = ((), (), s32[]{:S(2)}) async-start(), calls=%async_computation | async-start | bytes 33554432 | tf_op jit(solution)/shard_map/psum | solution.py:326
  22.0 71.9 %copy-start.90 = (f32[512]{0:T(512)}, f32[512]{0:T(512)S(1)}, u32[]{:S(2)}) copy-start(f32[512]{0:T(512)S(1)} %get-tuple-element.132) | copy-start | bytes 6148
  22.0 71.9 %copy-start.92 = (f32[512]{0:T(512)}, f32[512]{0:T(512)S(1)}, u32[]{:S(2)}) copy-start(f32[512]{0:T(512)S(1)} %get-tuple-element.133) | copy-start | bytes 6148
  24.3 14.0 %collective-permute-start = (bf16[320,1024]{1,0:T(8,128)(2,1)S(1)}, bf16[320,1024]{1,0:T(8,128)(2,1)}, u32[]{:S(2)}, u32[]{:S(2)}) collective-permute-start(bf16[320,1024]{1,0:T(8,128)(2,1)S(1)} %slice.288), channel_id=1, source_target_pairs={{0,1},{1,2},{2,3},{3,4},{4,5},{5,6},{6,7},{7,8},{8,9},{9,10},{10,1... | collective-permute-start | bytes 1966088 | tf_op jit(solution)/shard_map/ppermute | solution.py:25
  24.8 13.5 %collective-permute-start.1 = (bf16[320,1024]{1,0:T(8,128)(2,1)S(1)}, bf16[320,1024]{1,0:T(8,128)(2,1)}, u32[]{:S(2)}, u32[]{:S(2)}) collective-permute-start(bf16[320,1024]{1,0:T(8,128)(2,1)S(1)} %slice.288), channel_id=1, source_target_pairs={{1,0},{2,1},{3,2},{4,3},{5,4},{6,5},{7,6},{8,7},{9,8},{10,9},{11,1... | collective-permute-start | bytes 1966088 | tf_op jit(solution)/shard_map/ppermute | solution.py:27
  97.5 8.4 collective-permute-start.2
  105.5 11.6 copy-start.82
  105.5 11.6 copy-start.88
  105.5 97.2 %copy-start.78 = (f32[512]{0:T(512)}, f32[512]{0:T(512)S(1)}, u32[]{:S(2)}) copy-start(f32[512]{0:T(512)S(1)} %get-tuple-element.159) | copy-start | bytes 6148
  105.5 97.2 %copy-start.80 = (f32[512]{0:T(512)}, f32[512]{0:T(512)S(1)}, u32[]{:S(2)}) copy-start(f32[512]{0:T(512)S(1)} %get-tuple-element.160) | copy-start | bytes 6148
  107.4 84.7 %copy-start.1 = (f32[320,512]{1,0:T(8,128)}, f32[320,512]{1,0:T(8,128)S(1)}, u32[]{:S(2)}) copy-start(f32[320,512]{1,0:T(8,128)S(1)} %get-tuple-element.70) | copy-start | bytes 1966084
  111.0 22.0 %collective-permute-start.3 = (bf16[320,1024]{1,0:T(8,128)(2,1)}, bf16[320,1024]{1,0:T(8,128)(2,1)}, u32[]{:S(2)}, u32[]{:S(2)}) collective-permute-start(bf16[320,1024]{1,0:T(8,128)(2,1)} %slice.296), channel_id=1, source_target_pairs={{0,1},{1,2},{2,3},{3,4},{4,5},{5,6},{6,7},{7,8},{8,9},{9,10},{10,1... | collective-permute-start | bytes 1966088 | tf_op jit(solution)/shard_map/ppermute | solution.py:25
  116.3 16.7 %collective-permute-start.4 = (bf16[320,1024]{1,0:T(8,128)(2,1)}, bf16[320,1024]{1,0:T(8,128)(2,1)}, u32[]{:S(2)}, u32[]{:S(2)}) collective-permute-start(bf16[320,1024]{1,0:T(8,128)(2,1)} %slice.296), channel_id=1, source_target_pairs={{1,0},{2,1},{3,2},{4,3},{5,4},{6,5},{7,6},{8,7},{9,8},{10,9},{11,1... | collective-permute-start | bytes 1966088 | tf_op jit(solution)/shard_map/ppermute | solution.py:27
  119.8 96.4 %collective-permute-start.5 = (bf16[320,1024]{1,0:T(8,128)(2,1)}, bf16[320,1024]{1,0:T(8,128)(2,1)}, u32[]{:S(2)}, u32[]{:S(2)}) collective-permute-start(bf16[320,1024]{1,0:T(8,128)(2,1)} %slice.305), channel_id=1, source_target_pairs={{0,1},{1,2},{2,3},{3,4},{4,5},{5,6},{6,7},{7,8},{8,9},{9,10},{10,1... | collective-permute-start | bytes 1966088 | tf_op jit(solution)/shard_map/ppermute | solution.py:25
  120.3 95.8 %collective-permute-start.6 = (bf16[320,1024]{1,0:T(8,128)(2,1)}, bf16[320,1024]{1,0:T(8,128)(2,1)}, u32[]{:S(2)}, u32[]{:S(2)}) collective-permute-start(bf16[320,1024]{1,0:T(8,128)(2,1)} %slice.305), channel_id=1, source_target_pairs={{1,0},{2,1},{3,2},{4,3},{5,4},{6,5},{7,6},{8,7},{9,8},{10,9},{11,1... | collective-permute-start | bytes 1966088 | tf_op jit(solution)/shard_map/ppermute | solution.py:27
  192.6 15.2 %copy-start.4 = (f32[320,512]{1,0:T(8,128)}, f32[320,512]{1,0:T(8,128)S(1)}, u32[]{:S(2)}) copy-start(f32[320,512]{1,0:T(8,128)S(1)} %get-tuple-element.140) | copy-start | bytes 1966084
  195.8 82.0 %collective-permute-start.10 = (bf16[320,512]{1,0:T(8,128)(2,1)}, bf16[320,512]{1,0:T(8,128)(2,1)}, u32[]{:S(2)}, u32[]{:S(2)}) collective-permute-start(bf16[320,512]{1,0:T(8,128)(2,1)} %get-tuple-element.141), channel_id=1, source_target_pairs={{0,16},{1,17},{2,18},{3,19},{4,20},{5,21},{6,22},{7,23},{8,24},{9,... | collective-permute-start | bytes 983048 | tf_op jit(solution)/shard_map/ppermute | solution.py:37
  207.8 64.3 %copy-start.149 = (f32[320]{0:T(512)}, f32[320]{0:T(512)S(1)}, u32[]{:S(2)}) copy-start(f32[320]{0:T(512)S(1)} %get-tuple-element.24) | copy-start | bytes 3844
  208.3 68.1 %copy-start.18 = (f32[320,512]{1,0:T(8,128)}, f32[320,512]{1,0:T(8,128)S(1)}, u32[]{:S(2)}) copy-start(f32[320,512]{1,0:T(8,128)S(1)} %bitcast_add_fusion) | copy-start | bytes 1966084
  257.4 11.0 copy-start.35
  257.4 11.0 copy-start.70
  282.3 18.1 %collective-permute-start.11 = (bf16[320,1024]{1,0:T(8,128)(2,1)S(1)}, bf16[320,1024]{1,0:T(8,128)(2,1)}, u32[]{:S(2)}, u32[]{:S(2)}) collective-permute-start(bf16[320,1024]{1,0:T(8,128)(2,1)S(1)} %slice.314), channel_id=1, source_target_pairs={{0,1},{1,2},{2,3},{3,4},{4,5},{5,6},{6,7},{7,8},{8,9},{9,10},{10,1... | collective-permute-start | bytes 1966088 | tf_op jit(solution)/shard_map/ppermute | solution.py:25
  287.9 12.5 %collective-permute-start.12 = (bf16[320,1024]{1,0:T(8,128)(2,1)S(1)}, bf16[320,1024]{1,0:T(8,128)(2,1)}, u32[]{:S(2)}, u32[]{:S(2)}) collective-permute-start(bf16[320,1024]{1,0:T(8,128)(2,1)S(1)} %slice.314), channel_id=1, source_target_pairs={{1,0},{2,1},{3,2},{4,3},{5,4},{6,5},{7,6},{8,7},{9,8},{10,9},{11,1... | collective-permute-start | bytes 1966088 | tf_op jit(solution)/shard_map/ppermute | solution.py:27
  290.9 68.3 %collective-permute-start.13 = (bf16[320,1024]{1,0:T(8,128)(2,1)}, bf16[320,1024]{1,0:T(8,128)(2,1)}, u32[]{:S(2)}, u32[]{:S(2)}) collective-permute-start(bf16[320,1024]{1,0:T(8,128)(2,1)} %slice.323), channel_id=1, source_target_pairs={{0,1},{1,2},{2,3},{3,4},{4,5},{5,6},{6,7},{7,8},{8,9},{9,10},{10,1... | collective-permute-start | bytes 1966088 | tf_op jit(solution)/shard_map/ppermute | solution.py:25
  293.7 65.5 %collective-permute-start.14 = (bf16[320,1024]{1,0:T(8,128)(2,1)}, bf16[320,1024]{1,0:T(8,128)(2,1)}, u32[]{:S(2)}, u32[]{:S(2)}) collective-permute-start(bf16[320,1024]{1,0:T(8,128)(2,1)} %slice.323), channel_id=1, source_target_pairs={{1,0},{2,1},{3,2},{4,3},{5,4},{6,5},{7,6},{8,7},{9,8},{10,9},{11,1... | collective-permute-start | bytes 1966088 | tf_op jit(solution)/shard_map/ppermute | solution.py:27
  356.9 169.8 %copy-start.102 = (f32[320]{0:T(512)}, f32[320]{0:T(512)S(1)}, u32[]{:S(2)}) copy-start(f32[320]{0:T(512)S(1)} %broadcast_multiply_fusion.4) | copy-start | bytes 3844
  358.5 166.7 %copy-start.31 = (f32[320,512]{1,0:T(8,128)}, f32[320,512]{1,0:T(8,128)S(1)}, u32[]{:S(2)}) copy-start(f32[320,512]{1,0:T(8,128)S(1)} %get-tuple-element.65) | copy-start | bytes 1966084
  510.5 12.0 copy-start.141
  510.5 16.2 %copy-start.94 = (f32[512]{0:T(512)S(1)}, f32[512]{0:T(512)}, u32[]{:S(2)}) copy-start(f32[512]{0:T(512)} %get-tuple-element.121) | copy-start | bytes 6148
  510.5 16.2 %copy-start.95 = (f32[512]{0:T(512)S(1)}, f32[512]{0:T(512)}, u32[]{:S(2)}) copy-start(f32[512]{0:T(512)} %get-tuple-element.122) | copy-start | bytes 6148
  510.5 16.2 %copy-start.114 = (f32[320]{0:T(512)S(1)}, f32[320]{0:T(512)}, u32[]{:S(2)}) copy-start(f32[320]{0:T(512)} %add_rsqrt_fusion) | copy-start | bytes 3844
  511.6 19.2 %collective-permute-start.7 = (bf16[320,1024]{1,0:T(8,128)(2,1)}, bf16[320,1024]{1,0:T(8,128)(2,1)}, u32[]{:S(2)}, u32[]{:S(2)}) collective-permute-start(bf16[320,1024]{1,0:T(8,128)(2,1)} %get-tuple-element.89), channel_id=1, source_target_pairs={{0,1},{1,2},{2,3},{3,4},{4,5},{5,6},{6,7},{7,8},{8,9},{9,10},{10,1... | collective-permute-start | bytes 1966088 | tf_op jit(solution)/shard_map/ppermute | solution.py:25
  522.4 8.5 collective-permute-start.8
  536.6 151.9 %collective-permute-start.18 = (bf16[320,1024]{1,0:T(8,128)(2,1)}, bf16[320,1024]{1,0:T(8,128)(2,1)}, u32[]{:S(2)}, u32[]{:S(2)}) collective-permute-start(bf16[320,1024]{1,0:T(8,128)(2,1)} %slice.333), channel_id=1, source_target_pairs={{0,1},{1,2},{2,3},{3,4},{4,5},{5,6},{6,7},{7,8},{8,9},{9,10},{10,1... | collective-permute-start | bytes 1966088 | tf_op jit(solution)/shard_map/ppermute | solution.py:25
  544.3 144.2 %collective-permute-start.19 = (bf16[320,1024]{1,0:T(8,128)(2,1)}, bf16[320,1024]{1,0:T(8,128)(2,1)}, u32[]{:S(2)}, u32[]{:S(2)}) collective-permute-start(bf16[320,1024]{1,0:T(8,128)(2,1)} %slice.333), channel_id=1, source_target_pairs={{1,0},{2,1},{3,2},{4,3},{5,4},{6,5},{7,6},{8,7},{9,8},{10,9},{11,1... | collective-permute-start | bytes 1966088 | tf_op jit(solution)/shard_map/ppermute | solution.py:27
  545.6 11.2 collective-permute-start.9
  673.6 66.5 %collective-permute-start.15 = (bf16[320,1024]{1,0:T(8,128)(2,1)}, bf16[320,1024]{1,0:T(8,128)(2,1)}, u32[]{:S(2)}, u32[]{:S(2)}) collective-permute-start(bf16[320,1024]{1,0:T(8,128)(2,1)} %get-tuple-element.87), channel_id=1, source_target_pairs={{0,1},{1,2},{2,3},{3,4},{4,5},{5,6},{6,7},{7,8},{8,9},{9,10},{10,1... | collective-permute-start | bytes 1966088 | tf_op jit(solution)/shard_map/ppermute | solution.py:25
  675.2 65.0 %collective-permute-start.16 = (bf16[320,1024]{1,0:T(8,128)(2,1)}, bf16[320,1024]{1,0:T(8,128)(2,1)}, u32[]{:S(2)}, u32[]{:S(2)}) collective-permute-start(bf16[320,1024]{1,0:T(8,128)(2,1)} %get-tuple-element.88), channel_id=1, source_target_pairs={{1,0},{2,1},{3,2},{4,3},{5,4},{6,5},{7,6},{8,7},{9,8},{10,9},{11,1... | collective-permute-start | bytes 1966088 | tf_op jit(solution)/shard_map/ppermute | solution.py:27
  744.9 11.3 collective-permute-start.17
  871.4 16.6 %collective-permute-start.20 = (bf16[320,1024]{1,0:T(8,128)(2,1)S(1)}, bf16[320,1024]{1,0:T(8,128)(2,1)S(1)}, u32[]{:S(2)}, u32[]{:S(2)}) collective-permute-start(bf16[320,1024]{1,0:T(8,128)(2,1)S(1)} %get-tuple-element.85), channel_id=1, source_target_pairs={{0,1},{1,2},{2,3},{3,4},{4,5},{5,6},{6,7},{7,8},{8,9},{9,10},{10,1... | collective-permute-start | bytes 1966088 | tf_op jit(solution)/shard_map/ppermute | solution.py:25
  871.4 10.4 copy-start.37
  871.4 10.4 copy-start.48
  871.4 10.4 copy-start.63
  871.5 16.5 %collective-permute-start.21 = (bf16[320,1024]{1,0:T(8,128)(2,1)S(1)}, bf16[320,1024]{1,0:T(8,128)(2,1)S(1)}, u32[]{:S(2)}, u32[]{:S(2)}) collective-permute-start(bf16[320,1024]{1,0:T(8,128)(2,1)S(1)} %get-tuple-element.86), channel_id=1, source_target_pairs={{1,0},{2,1},{3,2},{4,3},{5,4},{6,5},{7,6},{8,7},{9,8},{10,9},{11,1... | collective-permute-start | bytes 1966088 | tf_op jit(solution)/shard_map/ppermute | solution.py:27
  898.0 63.1 %copy-start.152 = (f32[320]{0:T(512)S(1)}, f32[320]{0:T(512)}, u32[]{:S(2)}) copy-start(f32[320]{0:T(512)} %copy-done.151) | copy-start | bytes 3844
  898.1 64.5 %copy-start.42 = (f32[320,512]{1,0:T(8,128)S(1)}, f32[320,512]{1,0:T(8,128)}, u32[]{:S(2)}) copy-start(f32[320,512]{1,0:T(8,128)} %copy-done.40) | copy-start | bytes 1966084
  898.1 64.5 %copy-start.182 = (f32[1,512]{1,0:T(1,128)S(1)}, f32[1,512]{1,0:T(1,128)}, u32[]{:S(2)}) copy-start(f32[1,512]{1,0:T(1,128)} %param.25) | copy-start | bytes 6148
  (167 other events, 715.6 us)
Sparse Core Ops, SparseCore 0:
  898.2 299.8 all-reduce.3
where the time goes:
time: 1220 us
  local copies, waits for them, and re-layouts  362 us (30%)
  other arithmetic  267 us (22%)
  waiting for transfers between devices  246 us (20%)
  matrix products  200 us (16%)
  starting transfers between devices  66.8 us (5%)
  blocking collectives  61.7 us (5%)
  between operations  16.6 us (1%)
    psum x1, waiting for transfers between devices, shards(): lax.psum((ada_outer, ada_bias_sum, layer_sums[0], layer_sums[1], layer_su...  231 us
    scatter-add x3, other arithmetic, layer_backward(): jax.ops.segment_sum(grad_near.reshape(row_count * NEIGHBOURS, 2 * D), pla...  138 us
    unnamed x398, local copies, waits for them, and re-layouts  89.6 us
    gather x3, local copies, waits for them, and re-layouts, layer_backward(): near_rows = key_rim[places]  83.7 us
    gather x3, local copies, waits for them, and re-layouts, layer_tail(): near_rows = key_rim[places]  83.1 us
    psum x1, blocking collectives, shards(): lax.psum((ada_outer, ada_bias_sum, layer_sums[0], layer_sums[1], layer_su...  61.7 us
    dot_general x12, matrix products, rows_product(): lax.dot_general(left, right, (((0,), (0,)), ((), ())), preferred_element_...  41 us
    ppermute x9, starting transfers between devices, with_halo(): lax.ppermute(tail, axis, [(i, (i + 1) % count) for i in range(count)])  34.8 us
  transfers between devices with their start and end apart: 23, of which 5 were waited for; matrix products, arithmetic and copies ran while one was open for 36% of the time, Pallas kernels for 0%

commit v1 on v0

--- a/solution.py
+++ b/solution.py
@@ -73,86 +73,54 @@
     )
 
 
-def widen_rim(key_value):
-    return with_halo(key_value, (("wide", 0),), key_value.shape[0])
+def widen_rim(normed):
+    return with_halo(normed, (("wide", 0),), normed.shape[0])
 
 
 def pre_attention(layer_in, modulation, weights):
     normed_a = modulate(layer_in, modulation[:D], modulation[D : 2 * D]).astype(jnp.bfloat16)
-    mixed_qkv = jnp.dot(normed_a, weights[2], preferred_element_type=jnp.float32).astype(
-        jnp.bfloat16
-    )
-    return (normed_a, mixed_qkv, widen_rim(mixed_qkv[:, D:]))
-
-
-def head_scores(queries, near_rows, valid_slots):
-    scores = jnp.einsum(
-        "nhe,nkhe->nkh",
-        split_heads(queries),
-        split_heads(near_rows[:, :, :D]),
-        preferred_element_type=jnp.float32,
-    ) * HEAD_DIM ** (-0.5)
-    return jnp.where(valid_slots[:, :, None] > 0, scores, masked_score)
-
-
-def attention_forward(queries, near_rows, valid_slots):
-    row_count = queries.shape[0]
-    scores = head_scores(queries, near_rows, valid_slots)
-    row_top = jnp.max(scores, axis=1, keepdims=True)
-    raised = jnp.exp(scores - row_top)
-    total_weight = jnp.sum(raised, axis=1, keepdims=True)
-    soft_weights = raised / total_weight
-    attended = jnp.einsum(
-        "nkh,nkhe->nhe",
-        soft_weights,
-        split_heads(near_rows[:, :, D:]),
-        precision=lax.Precision.HIGHEST,
-        preferred_element_type=jnp.float32,
-    )
-    return (attended.reshape(row_count, D), row_top + jnp.log(total_weight))
-
-
-def attention_backward(queries, near_rows, valid_slots, log_total, grad_attended):
-    row_count = queries.shape[0]
-    soft_weights = jnp.exp(head_scores(queries, near_rows, valid_slots) - log_total)
-    key_heads = split_heads(near_rows[:, :, :D])
-    value_heads = split_heads(near_rows[:, :, D:])
-    query_heads = split_heads(queries).astype(jnp.float32)
-    grad_heads = split_heads(grad_attended)
-    grad_soft = jnp.einsum(
-        "nhe,nkhe->nkh",
-        grad_heads,
-        value_heads,
-        precision=lax.Precision.HIGHEST,
-        preferred_element_type=jnp.float32,
-    )
-    grad_values = soft_weights[:, :, :, None] * grad_heads[:, None, :, :]
-    grad_scores = (
-        soft_weights
-        * (grad_soft - jnp.sum(soft_weights * grad_soft, axis=1, keepdims=True))
-        * HEAD_DIM ** (-0.5)
-    )
-    grad_queries = jnp.einsum(
-        "nkh,nkhe->nhe",
-        grad_scores,
-        key_heads,
-        precision=lax.Precision.HIGHEST,
-        preferred_element_type=jnp.float32,
-    )
-    grad_keys = grad_scores[:, :, :, None] * query_heads[:, None, :, :]
-    grad_near = jnp.concatenate(
-        [
-            grad_keys.reshape(row_count, NEIGHBOURS, D),
-            grad_values.reshape(row_count, NEIGHBOURS, D),
-        ],
-        axis=2,
-    )
-    return (grad_queries.reshape(row_count, D), grad_near)
-
-
-def layer_tail(layer_in, modulation, weights, mixed_qkv, key_rim, places, valid_slots):
-    near_rows = key_rim[places]
-    attended, log_total = attention_forward(mixed_qkv[:, :D], near_rows, valid_slots)
+    window = widen_rim(normed_a)
+    queries = jnp.dot(normed_a, weights[2][:, :D], preferred_element_type=jnp.float32)
+    key_value = jnp.dot(window, weights[2][:, D:], preferred_element_type=jnp.float32)
+    return (window, queries.astype(jnp.bfloat16), key_value.astype(jnp.bfloat16))
+
+
+def heads_of(packed, start=0):
+    return [packed[:, start + h * HEAD_DIM : start + (h + 1) * HEAD_DIM] for h in range(HEADS)]
+
+
+def attention_forward(queries, key_value, counts):
+    attended, logs = [], []
+    for query, key, value in zip(heads_of(queries), heads_of(key_value), heads_of(key_value, D)):
+        scores = jnp.where(counts > 0, cross_product(query, key) * HEAD_DIM ** (-0.5), masked_score)
+        row_top = jnp.max(scores, axis=1, keepdims=True)
+        raised = jnp.exp(scores - row_top) * counts
+        total_weight = jnp.sum(raised, axis=1, keepdims=True)
+        part = jnp.dot(raised.astype(jnp.bfloat16), value, preferred_element_type=jnp.float32)
+        attended.append(part / total_weight)
+        logs.append(row_top + jnp.log(total_weight))
+    return jnp.concatenate(attended, axis=1), jnp.concatenate(logs, axis=1)
+
+
+def attention_backward(queries, key_value, counts, log_total, grad_attended):
+    grad_q, grad_k, grad_v = [], [], []
+    grad_low = grad_attended.astype(jnp.bfloat16)
+    for h, (query, key, value, grad) in enumerate(
+        zip(heads_of(queries), heads_of(key_value), heads_of(key_value, D), heads_of(grad_low))
+    ):
+        scores = cross_product(query, key) * HEAD_DIM ** (-0.5)
+        soft = jnp.where(counts > 0, jnp.exp(scores - log_total[:, h : h + 1]) * counts, 0.0)
+        grad_soft = cross_product(grad, value)
+        inner = jnp.sum(soft * grad_soft, axis=1, keepdims=True)
+        grad_scores = (soft * (grad_soft - inner) * HEAD_DIM ** (-0.5)).astype(jnp.bfloat16)
+        grad_q.append(jnp.dot(grad_scores, key, preferred_element_type=jnp.float32))
+        grad_k.append(rows_product(grad_scores, query))
+        grad_v.append(rows_product(soft.astype(jnp.bfloat16), grad))
+    return jnp.concatenate(grad_q, axis=1), jnp.concatenate(grad_k + grad_v, axis=1)
+
+
+def layer_tail(layer_in, modulation, weights, rim_parts, counts):
+    attended, log_total = attention_forward(rim_parts[1], rim_parts[2], counts)
     attended_low = attended.astype(jnp.bfloat16)
     mixed = layer_in + jnp.dot(attended_low, weights[3], preferred_element_type=jnp.float32)
     normed_b = modulate(mixed, modulation[2 * D : 3 * D], modulation[3 * D :]).astype(jnp.bfloat16)
@@ -163,12 +131,11 @@
 
 
 def layer_backward(
-    layer_in, modulation, weights, rim_parts, tail_parts, places, valid_slots, grad_out
+    layer_in, modulation, weights, rim_parts, tail_parts, counts, grad_out
 ):
-    normed_a, mixed_qkv, key_rim = rim_parts
+    window, queries, key_value = rim_parts
     attended_low, log_total, mixed, normed_b, hidden, active = tail_parts
     row_count = layer_in.shape[0]
-    near_rows = key_rim[places]
     grad_low = grad_out.astype(jnp.bfloat16)
     grad_down = rows_product(active, grad_low)
     grad_down_bias = jnp.sum(grad_out, axis=0)
@@ -184,24 +151,27 @@
     grad_mixed_low = grad_mixed.astype(jnp.bfloat16)
     grad_out_weight = rows_product(attended_low, grad_mixed_low)
     grad_attended = cross_product(grad_mixed_low, weights[3])
-    grad_queries, grad_near = attention_backward(
-        mixed_qkv[:, :D], near_rows, valid_slots, log_total, grad_attended
-    )
-    grad_rim = jax.ops.segment_sum(
-        grad_near.reshape(row_count * NEIGHBOURS, 2 * D),
-        places.reshape(-1),
-        num_segments=3 * row_count,
-    )
-    outer_rows = jnp.concatenate([grad_rim[:row_count], grad_rim[2 * row_count :]], axis=0)
-    returned = with_halo(outer_rows.astype(jnp.bfloat16), (("wide", 0),), row_count).astype(
-        outer_rows.dtype
-    )
-    grad_key_value = (
-        grad_rim[row_count : 2 * row_count] + returned[:row_count] + returned[3 * row_count :]
-    )
-    grad_qkv = jnp.concatenate([grad_queries, grad_key_value], axis=1).astype(jnp.bfloat16)
-    grad_qkv_weight = rows_product(normed_a, grad_qkv)
-    grad_normed_a = cross_product(grad_qkv, weights[2])
+    grad_queries, grad_key_value = attention_backward(
+        queries, key_value, counts, log_total, grad_attended
+    )
+    grad_queries = grad_queries.astype(jnp.bfloat16)
+    grad_key_value = grad_key_value.astype(jnp.bfloat16)
+    grad_qkv_weight = jnp.concatenate(
+        [
+            rows_product(window[row_count : 2 * row_count], grad_queries),
+            rows_product(window, grad_key_value),
+        ],
+        axis=1,
+    )
+    grad_window = cross_product(grad_key_value, weights[2][:, D:])
+    outer_rows = jnp.concatenate([grad_window[:row_count], grad_window[2 * row_count :]], axis=0)
+    returned = with_halo(outer_rows.astype(jnp.bfloat16), (("wide", 0),), row_count)
+    grad_normed_a = (
+        cross_product(grad_queries, weights[2][:, :D])
+        + grad_window[row_count : 2 * row_count]
+        + returned[:row_count].astype(jnp.float32)
+        + returned[3 * row_count :].astype(jnp.float32)
+    )
     norm_value_a, norm_back_a = jax.vjp(modulate, layer_in, modulation[:D], modulation[D : 2 * D])
     grad_in_part, grad_shift_a, grad_scale_a = norm_back_a(grad_normed_a)
     grad_in = grad_mixed + grad_in_part
@@ -250,10 +220,15 @@
     places = jnp.remainder(
         neighbours - (lax.axis_index("wide") - 1) * row_count, row_count * lax.axis_size("wide")
     )
+    columns = lax.broadcasted_iota(jnp.int32, (row_count, 3 * row_count), 1)
+    counts = jnp.zeros((row_count, 3 * row_count), jnp.float32)
+    for slot in range(NEIGHBOURS):
+        hit = (places[:, slot : slot + 1] == columns) & (valid_slots[:, slot : slot + 1] > 0)
+        counts = counts + hit.astype(jnp.float32)
     blank = jnp.zeros((row_count, D), jnp.float32)
     blank_tail = (
         jnp.zeros((row_count, D), jnp.bfloat16),
-        jnp.zeros((row_count, 1, HEADS), jnp.float32),
+        jnp.zeros((row_count, HEADS), jnp.float32),
         jnp.zeros((row_count, D), jnp.float32),
         jnp.zeros((row_count, D), jnp.bfloat16),
         jnp.zeros((row_count, FF), jnp.float32),
@@ -266,8 +241,7 @@
     arriving = jnp.zeros((row_count, D), jnp.bfloat16)
     returning = jnp.zeros((row_count, D), jnp.bfloat16)
     layer_sums = tuple((jnp.zeros(member.shape, jnp.float32) for member in weights[2:]))
-    ada_outer = jnp.zeros(weights[0].shape, jnp.float32)
-    ada_bias_sum = jnp.zeros((4 * D,), jnp.float32)
+    modulation_grads = []
 
     def pick_embed(position):
         return sigma_embed[jnp.clip(position, 0, MICRO - 1)]
@@ -279,7 +253,7 @@
             modulation = make_modulation(weights, pick_embed(moment - section_index))
             rim_parts = pre_attention(layer_in, modulation, weights)
             output, tail_parts = layer_tail(
-                layer_in, modulation, weights, rim_parts[1], rim_parts[2], places, valid_slots
+                layer_in, modulation, weights, rim_parts, counts
             )
             inputs_kept.append(layer_in)
             tails_kept.append(tail_parts)
@@ -307,7 +281,7 @@
             sent_down = cotangent[moment - 1] if moment <= MICRO else blank
             grad_out = jnp.where(first_section, returning.astype(jnp.float32), sent_down)
             grad_in, grad_mod, layer_grads = layer_backward(
-                layer_in, modulation, weights, rim_parts, tail_parts, places, valid_slots, grad_out
+                layer_in, modulation, weights, rim_parts, tail_parts, counts, grad_out
             )
             input_grads.append(grad_in)
             if moment <= MICRO:
@@ -315,30 +289,31 @@
             layer_sums = tuple(
                 (running + addend for running, addend in zip(layer_sums, layer_grads))
             )
-            ada_outer = ada_outer + embed_row.astype(jnp.float32)[:, None] * grad_mod[None, :]
-            ada_bias_sum = ada_bias_sum + grad_mod
+            modulation_grads.append(grad_mod)
     boundary = jnp.stack(
         [
             jnp.where(first_section, input_grads[position + 2], outputs[position + 1])
             for position in range(MICRO)
         ]
     )
+    modulation_parts = jnp.stack(
+        [
+            jnp.where(first_section, modulation_grads[position + 1], modulation_grads[position])
+            for position in range(MICRO)
+        ]
+    )
+    modulation_sums, up_bias_sum, down_bias_sum = lax.psum(
+        (modulation_parts, layer_sums[3], layer_sums[5]), "wide"
+    )
     summed = lax.psum(
-        (
-            ada_outer,
-            ada_bias_sum,
-            layer_sums[0],
-            layer_sums[1],
-            layer_sums[2],
-            layer_sums[3],
-            layer_sums[4],
-            layer_sums[5],
-        ),
-        "wide",
-    )
-    grad_ada_weight = summed[0]
-    grad_ada_bias = summed[1]
-    remaining = summed[2:]
+        tuple(layer_sums[k].astype(jnp.bfloat16) for k in (0, 1, 2, 4)), "wide"
+    )
+    summed = tuple(member.astype(jnp.float32) for member in summed)
+    grad_ada_weight = jnp.sum(
+        sigma_embed.astype(jnp.float32)[:, :, None] * modulation_sums[:, None, :], axis=0
+    )
+    grad_ada_bias = jnp.sum(modulation_sums, axis=0)
+    remaining = (summed[0], summed[1], summed[2], up_bias_sum, summed[3], down_bias_sum)
     return (
         boundary[None],
         grad_ada_weight[None],

time: 1220 us -> 381 us (0.31)
  local copies, waits for them, and re-layouts: 362 us -> 4.3 us
  other arithmetic: 267 us -> 41 us
  waiting for transfers between devices: 246 us -> 84.9 us
  matrix products: 200 us -> 118 us
  starting transfers between devices: 66.8 us -> 53.8 us
    gather x6 -> x0, local copies, waits for them, and re-layouts: 167 us -> none  [the longest x3 83.7 us: layer_backward(): near_rows = key_rim[places]]
    psum x1, waiting for transfers between devices: 231 us -> 67.7 us  [shards(): lax.psum(tuple((layer_sums[k].astype(jnp.bfloat16) for k in (0, 1, 2, 4))...]
    scatter-add x3 -> x0, other arithmetic: 138 us -> none  [layer_backward(): jax.ops.segment_sum(grad_near.reshape(row_count * NEIGHBOURS, 2 * D), pla...]
    dot_general x21 -> x36, matrix products: 114 us -> 20.6 us  [the longest x6 8.26 us: pre_attention(): jnp.dot(window, weights[2][:, D:], preferred_element_type=jnp.float32)]
    unnamed x398 -> x72, local copies, waits for them, and re-layouts: 89.6 us -> 3.12 us
    mul x12 -> x0, local copies, waits for them, and re-layouts: 57 us -> none  [the longest x3 21.4 us: attention_backward(): grad_keys = grad_scores[:, :, :, None] * query_heads[:, None, :, :]]
    mul x6 -> x0, other arithmetic: 56.6 us -> none  [the longest x3 28.7 us: attention_backward(): grad_values = soft_weights[:, :, :, None] * grad_heads[:, None, :, :]]
    ppermute x9, starting transfers between devices: 34.8 us -> 0.85 us  [with_halo(): lax.ppermute(tail, axis, [(i, (i + 1) % count) for i in range(count)])]
  transfers between devices with their start and end apart: 23 -> 23, of which waited for: 5 -> 4; matrix products, arithmetic and copies ran while one was open for 36% -> 25% of each run, Pallas kernels for 0% -> 0%
where the time goes in v1:
time: 381 us; the launch traced here: 378 us
  matrix products  118 us (31%)
  waiting for transfers between devices  84.9 us (22%)
  blocking collectives  60.5 us (16%)
  starting transfers between devices  53.8 us (14%)
  other arithmetic  41 us (11%)
  between operations  16.1 us (4%)
  local copies, waits for them, and re-layouts  4.3 us (1%)
    psum x1, waiting for transfers between devices, shards(): lax.psum(tuple((layer_sums[k].astype(jnp.bfloat16) for k in (0, 1, 2, 4))...  67.7 us
    psum x1, blocking collectives, shards(): lax.psum((modulation_parts, layer_sums[3], layer_sums[5]), 'wide')  60.5 us
    ppermute x9, starting transfers between devices, with_halo(): lax.ppermute(head, axis, [((i + 1) % count, i) for i in range(count)])  41.2 us
    dot_general x39, matrix products, rows_product(): lax.dot_general(left, right, (((0,), (0,)), ((), ())), preferred_element_...  39.8 us
    dot_general x51, matrix products, cross_product(): lax.dot_general(left, right, (((1,), (1,)), ((), ())), preferred_element_...  38 us
    ppermute x4, waiting for transfers between devices, shifted(): lax.ppermute(value, axis, [(source, source + steps) for source in range(f...  14.2 us
    ppermute x4, starting transfers between devices, shifted(): lax.ppermute(value, axis, [(source, source + steps) for source in range(f...  11.7 us
    dot_general x6, matrix products, make_modulation(): jnp.dot(embed_row[None, :], weights[0], preferred_element_type=jnp.float32)  10.5 us
  transfers between devices with their start and end apart: 23, of which 4 were waited for; matrix products, arithmetic and copies ran while one was open for 25% of the time, Pallas kernels for 0%

profile of v1, /device:TPU:0, one launch (start us, length us, event | category | flops | bytes accessed | tf_op | source)
XLA Modules:
  0.0 378.1 jit_solution(202520727689022303)
XLA Ops:
  7.3 1.4 fusion.253
  8.6 1.3 multiply_reduce_fusion.36
  10.0 2.1 fusion.30
  12.6 2.0 fusion.26
  14.6 2.0 fusion.22
  16.5 2.0 fusion.32
  18.5 2.1 fusion.24
  22.0 5.2 %collective-permute-start.1 = (bf16[320,512]{1,0:T(8,128)(2,1)}, bf16[320,512]{1,0:T(8,128)(2,1)}, u32[]{:S(2)}, u32[]{:S(2)}) collective-permute-start(bf16[320,512]{1,0:T(8,128)(2,1)} %add_convert_fusion.11), channel_id=1, source_target_pairs={{1,0},{2,1},{3,2},{4,3},{5,4},{6,5},{7,6},{8,7},{9,8},{10,9},{11,1... | collective-permute-start | bytes 983048 | tf_op jit(solution)/shard_map/ppermute | solution.py:27
  28.6 3.7 broadcast_compare_fusion
  33.1 1.5 convolution_convert_fusion.14
  34.6 2.4 convolution_convert_fusion.5
  38.9 1.3 fusion.361
  46.0 4.0 %collective-permute-start.2 = (bf16[320,512]{1,0:T(8,128)(2,1)S(1)}, bf16[320,512]{1,0:T(8,128)(2,1)S(1)}, u32[]{:S(2)}, u32[]{:S(2)}) collective-permute-start(bf16[320,512]{1,0:T(8,128)(2,1)S(1)} %fusion.157), channel_id=1, source_target_pairs={{0,16},{1,17},{2,18},{3,19},{4,20},{5,21},{6,22},{7,23},{8,24},{9,... | collective-permute-start | bytes 983048 | tf_op jit(solution)/shard_map/ppermute | solution.py:37
  50.1 7.2 %collective-permute-done.2 = bf16[320,512]{1,0:T(8,128)(2,1)S(1)} collective-permute-done((bf16[320,512]{1,0:T(8,128)(2,1)S(1)}, bf16[320,512]{1,0:T(8,128)(2,1)S(1)}, u32[]{:S(2)}, u32[]{:S(2)}) %collective-permute-start.2) | collective-permute-done | bytes 327712 | tf_op jit(solution)/shard_map/ppermute | solution.py:37
  58.3 4.4 %collective-permute-start.4 = (bf16[320,512]{1,0:T(8,128)(2,1)S(1)}, bf16[320,512]{1,0:T(8,128)(2,1)S(1)}, u32[]{:S(2)}, u32[]{:S(2)}) collective-permute-start(bf16[320,512]{1,0:T(8,128)(2,1)S(1)} %get-tuple-element.136), channel_id=1, source_target_pairs={{1,0},{2,1},{3,2},{4,3},{5,4},{6,5},{7,6},{8,7},{9,8},{10,9},{11,1... | collective-permute-start | bytes 983048 | tf_op jit(solution)/shard_map/ppermute | solution.py:27
  63.1 4.9 %collective-permute-start.6 = (bf16[320,512]{1,0:T(8,128)(2,1)S(1)}, bf16[320,512]{1,0:T(8,128)(2,1)S(1)}, u32[]{:S(2)}, u32[]{:S(2)}) collective-permute-start(bf16[320,512]{1,0:T(8,128)(2,1)S(1)} %get-tuple-element.135), channel_id=1, source_target_pairs={{1,0},{2,1},{3,2},{4,3},{5,4},{6,5},{7,6},{8,7},{9,8},{10,9},{11,1... | collective-permute-start | bytes 983048 | tf_op jit(solution)/shard_map/ppermute | solution.py:27
  77.2 2.1 convert_reduce_fusion.2
  86.0 3.4 fusion.116
  89.3 1.4 fusion.259
  91.2 4.4 %collective-permute-start.10 = (bf16[320,512]{1,0:T(8,128)(2,1)S(1)}, bf16[320,512]{1,0:T(8,128)(2,1)S(1)}, u32[]{:S(2)}, u32[]{:S(2)}) collective-permute-start(bf16[320,512]{1,0:T(8,128)(2,1)S(1)} %get-tuple-element.200), channel_id=1, source_target_pairs={{0,16},{1,17},{2,18},{3,19},{4,20},{5,21},{6,22},{7,23},{8,24},{9,... | collective-permute-start | bytes 983048 | tf_op jit(solution)/shard_map/ppermute | solution.py:37
  104.4 4.4 %collective-permute-start.8 = (bf16[320,512]{1,0:T(8,128)(2,1)S(1)}, bf16[320,512]{1,0:T(8,128)(2,1)S(1)}, u32[]{:S(2)}, u32[]{:S(2)}) collective-permute-start(bf16[320,512]{1,0:T(8,128)(2,1)S(1)} %get-tuple-element.132), channel_id=1, source_target_pairs={{1,0},{2,1},{3,2},{4,3},{5,4},{6,5},{7,6},{8,7},{9,8},{10,9},{11,1... | collective-permute-start | bytes 983048 | tf_op jit(solution)/shard_map/ppermute | solution.py:27
  111.4 4.4 %collective-permute-start.12 = (bf16[320,512]{1,0:T(8,128)(2,1)S(1)}, bf16[320,512]{1,0:T(8,128)(2,1)S(1)}, u32[]{:S(2)}, u32[]{:S(2)}) collective-permute-start(bf16[320,512]{1,0:T(8,128)(2,1)S(1)} %get-tuple-element.139), channel_id=1, source_target_pairs={{1,0},{2,1},{3,2},{4,3},{5,4},{6,5},{7,6},{8,7},{9,8},{10,9},{11,1... | collective-permute-start | bytes 983048 | tf_op jit(solution)/shard_map/ppermute | solution.py:27
  117.0 4.5 %collective-permute-start.14 = (bf16[320,512]{1,0:T(8,128)(2,1)S(1)}, bf16[320,512]{1,0:T(8,128)(2,1)S(1)}, u32[]{:S(2)}, u32[]{:S(2)}) collective-permute-start(bf16[320,512]{1,0:T(8,128)(2,1)S(1)} %add_convert_fusion.3), channel_id=1, source_target_pairs={{1,0},{2,1},{3,2},{4,3},{5,4},{6,5},{7,6},{8,7},{9,8},{10,9},{11,1... | collective-permute-start | bytes 983048 | tf_op jit(solution)/shard_map/ppermute | solution.py:27
  123.3 4.5 %collective-permute-start.19 = (bf16[320,512]{1,0:T(8,128)(2,1)S(1)}, bf16[320,512]{1,0:T(8,128)(2,1)S(1)}, u32[]{:S(2)}, u32[]{:S(2)}) collective-permute-start(bf16[320,512]{1,0:T(8,128)(2,1)S(1)} %get-tuple-element.134), channel_id=1, source_target_pairs={{1,0},{2,1},{3,2},{4,3},{5,4},{6,5},{7,6},{8,7},{9,8},{10,9},{11,1... | collective-permute-start | bytes 983048 | tf_op jit(solution)/shard_map/ppermute | solution.py:27
  127.8 1.7 collective-permute-start.9
  132.7 1.3 fusion.369
  137.7 1.5 convert_reduce_fusion.1
  145.8 1.5 fusion.257
  155.9 6.7 %fusion.114 = f32[2048,512]{1,0:T(8,128)} fusion(pred[]{:T(512)S(6)} %eq.165, f32[2,320,512]{2,1,0:T(8,128)S(1)} %copy-done.5, bf16[320,512]{1,0:T(8,128)(2,1)S(1)} %collective-permute-done.9, f32[320,2048]{1,0:T(8,128)} %copy-done.33, f32[320,2048]{1,0:T(8,128)} %copy-done.34), kind=kOutput, calls=%fused_computation.157 | convolution fusion | flops 678625280 | bytes 10093568 | tf_op jit(solution)/shard_map/dot_general | solution.py:55
  164.3 4.5 %collective-permute-start.16 = (bf16[320,512]{1,0:T(8,128)(2,1)S(1)}, bf16[320,512]{1,0:T(8,128)(2,1)S(1)}, u32[]{:S(2)}, u32[]{:S(2)}) collective-permute-start(bf16[320,512]{1,0:T(8,128)(2,1)S(1)} %get-tuple-element.130), channel_id=1, source_target_pairs={{1,0},{2,1},{3,2},{4,3},{5,4},{6,5},{7,6},{8,7},{9,8},{10,9},{11,1... | collective-permute-start | bytes 983048 | tf_op jit(solution)/shard_map/ppermute | solution.py:27
  170.3 3.0 collective-permute-done.16
  175.4 1.6 collective-permute-start.17
  177.5 7.0 %collective-permute-done.17 = bf16[320,512]{1,0:T(8,128)(2,1)S(1)} collective-permute-done((bf16[320,512]{1,0:T(8,128)(2,1)S(1)}, bf16[320,512]{1,0:T(8,128)(2,1)S(1)}, u32[]{:S(2)}, u32[]{:S(2)}) %collective-permute-start.17) | collective-permute-done | bytes 327712 | tf_op jit(solution)/shard_map/ppermute | solution.py:37
  184.5 1.5 convert_reduce_fusion
  200.1 2.5 fusion.541
  203.5 4.4 %collective-permute-start.21 = (bf16[320,512]{1,0:T(8,128)(2,1)}, bf16[320,512]{1,0:T(8,128)(2,1)}, u32[]{:S(2)}, u32[]{:S(2)}) collective-permute-start(bf16[320,512]{1,0:T(8,128)(2,1)} %get-tuple-element.128), channel_id=1, source_target_pairs={{1,0},{2,1},{3,2},{4,3},{5,4},{6,5},{7,6},{8,7},{9,8},{10,9},{11,1... | collective-permute-start | bytes 983048 | tf_op jit(solution)/shard_map/ppermute | solution.py:27
  208.0 2.7 fusion.2
  212.5 2.1 fusion.46
  215.2 4.9 %fusion.3 = bf16[1,2048,512]{2,1,0:T(8,128)(2,1)} fusion(f32[2048,512]{1,0:T(8,128)S(1)} %copy-done.35, f32[2048,512]{1,0:T(8,128)} %fusion.114, pred[]{:T(512)S(6)} %eq.165, bf16[320,512]{1,0:T(8,128)(2,1)S(1)} %collective-permute-done.17, f32[320,2048]{1,0:T(8,128)S(1)} %copy-done.32), kind=kOutput, calls=%fused_computation.13 | convolution fusion | flops 678658048 | bytes 13434881 | tf_op jit(solution)/shard_map/dot_general | solution.py:55
  220.9 3.0 multiply_reduce_fusion.14
  223.9 60.5 %all-reduce = (f32[2,2048]{1,0:T(2,128)S(1)}, f32[1,2048]{1,0:T(1,128)}, f32[1,512]{1,0:T(1,128)}) all-reduce(f32[2,2048]{1,0:T(2,128)S(1)} %pad_maximum_fusion.31, f32[1,2048]{1,0:T(1,128)S(1)} %bitcast.239, f32[1,512]{1,0:T(1,128)S(1)} %bitcast.241), channel_id=1, replica_groups=mesh['section'=2,'wide'=16] {'wide'}, use_global_device_ids=true, to_apply=%region_84.85 | all-reduce | flops 6656 | bytes 53248 | tf_op jit(solution)/shard_map/psum | solution.py:305
  285.1 1.5 fusion.512
  286.6 2.8 select_bitcast_fusion
  290.6 2.5 multiply_reduce_fusion
  293.1 67.7 %all-reduce.4.cloned.1.call-done = (bf16[1,512,1536]{2,1,0:T(8,128)(2,1)}, bf16[1,512,512]{2,1,0:T(8,128)(2,1)}, bf16[1,512,2048]{2,1,0:T(8,128)(2,1)}, bf16[1,2048,512]{2,1,0:T(8,128)(2,1)}) async-done(((bf16[1,512,1536]{2,1,0:T(8,128)(2,1)}, bf16[1,512,512]{2,1,0:T(8,128)(2,1)}, bf16[1,512,2048]{2,1,0:T(8,128)(2,1)}, bf16[1,2048,512]{2,1,0:T(8,128)(2,1)}), (bf16[1,512,1536]{2,1,0:T(8,128)(2,1)}, ...) | async-done | bytes 6291472 | tf_op jit(solution)/shard_map/psum | solution.py:308
  360.8 4.3 %broadcast_in_dim.110 = f32[1,512,2048]{2,1,0:T(8,128)} convert(bf16[1,512,2048]{2,1,0:T(8,128)(2,1)} %get-tuple-element.100) | non-fusion elementwise | flops 1048576 | bytes 6291456 | tf_op jit(solution)/shard_map/broadcast_in_dim | solution.py:323
  365.1 2.6 broadcast_in_dim.114
  367.7 2.1 broadcast_in_dim.106
  (344 shorter events, 91.8 us)
Async XLA Ops:
  7.2 38.0 %copy-start = (bf16[1,2048,512]{2,1,0:T(8,128)(2,1)S(1)}, bf16[1,2048,512]{2,1,0:T(8,128)(2,1)}, u32[]{:S(2)}) copy-start(bf16[1,2048,512]{2,1,0:T(8,128)(2,1)} %param.24) | copy-start | bytes 6291460
  7.2 2.8 copy-start.14
  7.2 353.6 %all-reduce.4.cloned.1.call-start = ((), (), s32[]{:S(2)}) async-start(), calls=%async_computation | async-start | bytes 12582912 | tf_op jit(solution)/shard_map/psum | solution.py:308
  10.0 2.2 copy-start.1
  18.5 2.1 copy-start.2
  18.5 2.1 copy-start.21
  18.5 9.3 %copy-start.15 = (s32[320,16]{0,1:T(8,128)S(1)}, s32[320,16]{0,1:T(8,128)}, u32[]{:S(2)}) copy-start(s32[320,16]{0,1:T(8,128)} %param.16) | copy-start | bytes 61444
  18.5 9.4 %copy-start.16 = (s32[320,16]{0,1:T(8,128)S(1)}, s32[320,16]{0,1:T(8,128)}, u32[]{:S(2)}) copy-start(s32[320,16]{0,1:T(8,128)} %param.17) | copy-start | bytes 61444
  21.6 13.0 %collective-permute-start = (bf16[320,512]{1,0:T(8,128)(2,1)}, bf16[320,512]{1,0:T(8,128)(2,1)}, u32[]{:S(2)}, u32[]{:S(2)}) collective-permute-start(bf16[320,512]{1,0:T(8,128)(2,1)} %add_convert_fusion.11), channel_id=1, source_target_pairs={{0,1},{1,2},{2,3},{3,4},{4,5},{5,6},{6,7},{7,8},{8,9},{9,10},{10,1... | collective-permute-start | bytes 983048 | tf_op jit(solution)/shard_map/ppermute | solution.py:25
  22.0 12.5 %collective-permute-start.1 = (bf16[320,512]{1,0:T(8,128)(2,1)}, bf16[320,512]{1,0:T(8,128)(2,1)}, u32[]{:S(2)}, u32[]{:S(2)}) collective-permute-start(bf16[320,512]{1,0:T(8,128)(2,1)} %add_convert_fusion.11), channel_id=1, source_target_pairs={{1,0},{2,1},{3,2},{4,3},{5,4},{6,5},{7,6},{8,7},{9,8},{10,9},{11,1... | collective-permute-start | bytes 983048 | tf_op jit(solution)/shard_map/ppermute | solution.py:27
  27.8 4.6 %copy-start.5 = (f32[2,320,512]{2,1,0:T(8,128)S(1)}, f32[2,320,512]{2,1,0:T(8,128)}, u32[]{:S(2)}) copy-start(f32[2,320,512]{2,1,0:T(8,128)} %param.15) | copy-start | bytes 3932164
  32.4 2.2 copy-start.23
  45.1 92.6 %copy-start.33 = (f32[320,2048]{1,0:T(8,128)}, f32[320,2048]{1,0:T(8,128)S(1)}, u32[]{:S(2)}) copy-start(f32[320,2048]{1,0:T(8,128)S(1)} %convolution_add_fusion.2) | copy-start | bytes 7864324
  45.1 12.1 %copy-start.3 = (f32[2,320,512]{2,1,0:T(8,128)S(1)}, f32[2,320,512]{2,1,0:T(8,128)}, u32[]{:S(2)}) copy-start(f32[2,320,512]{2,1,0:T(8,128)} %param.13) | copy-start | bytes 3932164
  46.0 11.2 %collective-permute-start.2 = (bf16[320,512]{1,0:T(8,128)(2,1)S(1)}, bf16[320,512]{1,0:T(8,128)(2,1)S(1)}, u32[]{:S(2)}, u32[]{:S(2)}) collective-permute-start(bf16[320,512]{1,0:T(8,128)(2,1)S(1)} %fusion.157), channel_id=1, source_target_pairs={{0,16},{1,17},{2,18},{3,19},{4,20},{5,21},{6,22},{7,23},{8,24},{9,... | collective-permute-start | bytes 983048 | tf_op jit(solution)/shard_map/ppermute | solution.py:37
  58.2 10.1 %collective-permute-start.3 = (bf16[320,512]{1,0:T(8,128)(2,1)S(1)}, bf16[320,512]{1,0:T(8,128)(2,1)S(1)}, u32[]{:S(2)}, u32[]{:S(2)}) collective-permute-start(bf16[320,512]{1,0:T(8,128)(2,1)S(1)} %get-tuple-element.136), channel_id=1, source_target_pairs={{0,1},{1,2},{2,3},{3,4},{4,5},{5,6},{6,7},{7,8},{8,9},{9,10},{10,1... | collective-permute-start | bytes 983048 | tf_op jit(solution)/shard_map/ppermute | solution.py:25
  58.3 10.1 %collective-permute-start.4 = (bf16[320,512]{1,0:T(8,128)(2,1)S(1)}, bf16[320,512]{1,0:T(8,128)(2,1)S(1)}, u32[]{:S(2)}, u32[]{:S(2)}) collective-permute-start(bf16[320,512]{1,0:T(8,128)(2,1)S(1)} %get-tuple-element.136), channel_id=1, source_target_pairs={{1,0},{2,1},{3,2},{4,3},{5,4},{6,5},{7,6},{8,7},{9,8},{10,9},{11,1... | collective-permute-start | bytes 983048 | tf_op jit(solution)/shard_map/ppermute | solution.py:27
  63.0 18.3 %collective-permute-start.5 = (bf16[320,512]{1,0:T(8,128)(2,1)S(1)}, bf16[320,512]{1,0:T(8,128)(2,1)S(1)}, u32[]{:S(2)}, u32[]{:S(2)}) collective-permute-start(bf16[320,512]{1,0:T(8,128)(2,1)S(1)} %get-tuple-element.135), channel_id=1, source_target_pairs={{0,1},{1,2},{2,3},{3,4},{4,5},{5,6},{6,7},{7,8},{8,9},{9,10},{10,1... | collective-permute-start | bytes 983048 | tf_op jit(solution)/shard_map/ppermute | solution.py:25
  63.1 18.2 %collective-permute-start.6 = (bf16[320,512]{1,0:T(8,128)(2,1)S(1)}, bf16[320,512]{1,0:T(8,128)(2,1)S(1)}, u32[]{:S(2)}, u32[]{:S(2)}) collective-permute-start(bf16[320,512]{1,0:T(8,128)(2,1)S(1)} %get-tuple-element.135), channel_id=1, source_target_pairs={{1,0},{2,1},{3,2},{4,3},{5,4},{6,5},{7,6},{8,7},{9,8},{10,9},{11,1... | collective-permute-start | bytes 983048 | tf_op jit(solution)/shard_map/ppermute | solution.py:27
  76.3 9.7 %copy-start.31 = (f32[320,2048]{1,0:T(8,128)}, f32[320,2048]{1,0:T(8,128)S(1)}, u32[]{:S(2)}) copy-start(f32[320,2048]{1,0:T(8,128)S(1)} %convolution_add_fusion.1) | copy-start | bytes 7864324
  91.2 19.4 %collective-permute-start.10 = (bf16[320,512]{1,0:T(8,128)(2,1)S(1)}, bf16[320,512]{1,0:T(8,128)(2,1)S(1)}, u32[]{:S(2)}, u32[]{:S(2)}) collective-permute-start(bf16[320,512]{1,0:T(8,128)(2,1)S(1)} %get-tuple-element.200), channel_id=1, source_target_pairs={{0,16},{1,17},{2,18},{3,19},{4,20},{5,21},{6,22},{7,23},{8,24},{9,... | collective-permute-start | bytes 983048 | tf_op jit(solution)/shard_map/ppermute | solution.py:37
  104.3 12.7 %collective-permute-start.7 = (bf16[320,512]{1,0:T(8,128)(2,1)S(1)}, bf16[320,512]{1,0:T(8,128)(2,1)S(1)}, u32[]{:S(2)}, u32[]{:S(2)}) collective-permute-start(bf16[320,512]{1,0:T(8,128)(2,1)S(1)} %get-tuple-element.131), channel_id=1, source_target_pairs={{0,1},{1,2},{2,3},{3,4},{4,5},{5,6},{6,7},{7,8},{8,9},{9,10},{10,1... | collective-permute-start | bytes 983048 | tf_op jit(solution)/shard_map/ppermute | solution.py:25
  104.4 17.1 %collective-permute-start.8 = (bf16[320,512]{1,0:T(8,128)(2,1)S(1)}, bf16[320,512]{1,0:T(8,128)(2,1)S(1)}, u32[]{:S(2)}, u32[]{:S(2)}) collective-permute-start(bf16[320,512]{1,0:T(8,128)(2,1)S(1)} %get-tuple-element.132), channel_id=1, source_target_pairs={{1,0},{2,1},{3,2},{4,3},{5,4},{6,5},{7,6},{8,7},{9,8},{10,9},{11,1... | collective-permute-start | bytes 983048 | tf_op jit(solution)/shard_map/ppermute | solution.py:27
  111.3 12.0 %collective-permute-start.11 = (bf16[320,512]{1,0:T(8,128)(2,1)S(1)}, bf16[320,512]{1,0:T(8,128)(2,1)S(1)}, u32[]{:S(2)}, u32[]{:S(2)}) collective-permute-start(bf16[320,512]{1,0:T(8,128)(2,1)S(1)} %get-tuple-element.139), channel_id=1, source_target_pairs={{0,1},{1,2},{2,3},{3,4},{4,5},{5,6},{6,7},{7,8},{8,9},{9,10},{10,1... | collective-permute-start | bytes 983048 | tf_op jit(solution)/shard_map/ppermute | solution.py:25
  111.4 16.4 %collective-permute-start.12 = (bf16[320,512]{1,0:T(8,128)(2,1)S(1)}, bf16[320,512]{1,0:T(8,128)(2,1)S(1)}, u32[]{:S(2)}, u32[]{:S(2)}) collective-permute-start(bf16[320,512]{1,0:T(8,128)(2,1)S(1)} %get-tuple-element.139), channel_id=1, source_target_pairs={{1,0},{2,1},{3,2},{4,3},{5,4},{6,5},{7,6},{8,7},{9,8},{10,9},{11,1... | collective-permute-start | bytes 983048 | tf_op jit(solution)/shard_map/ppermute | solution.py:27
  116.6 24.6 %collective-permute-start.13 = (bf16[320,512]{1,0:T(8,128)(2,1)S(1)}, bf16[320,512]{1,0:T(8,128)(2,1)S(1)}, u32[]{:S(2)}, u32[]{:S(2)}) collective-permute-start(bf16[320,512]{1,0:T(8,128)(2,1)S(1)} %add_convert_fusion.3), channel_id=1, source_target_pairs={{0,1},{1,2},{2,3},{3,4},{4,5},{5,6},{6,7},{7,8},{8,9},{9,10},{10,1... | collective-permute-start | bytes 983048 | tf_op jit(solution)/shard_map/ppermute | solution.py:25
  117.0 24.2 %collective-permute-start.14 = (bf16[320,512]{1,0:T(8,128)(2,1)S(1)}, bf16[320,512]{1,0:T(8,128)(2,1)S(1)}, u32[]{:S(2)}, u32[]{:S(2)}) collective-permute-start(bf16[320,512]{1,0:T(8,128)(2,1)S(1)} %add_convert_fusion.3), channel_id=1, source_target_pairs={{1,0},{2,1},{3,2},{4,3},{5,4},{6,5},{7,6},{8,7},{9,8},{10,9},{11,1... | collective-permute-start | bytes 983048 | tf_op jit(solution)/shard_map/ppermute | solution.py:27
  122.8 46.3 %collective-permute-start.18 = (bf16[320,512]{1,0:T(8,128)(2,1)S(1)}, bf16[320,512]{1,0:T(8,128)(2,1)S(1)}, u32[]{:S(2)}, u32[]{:S(2)}) collective-permute-start(bf16[320,512]{1,0:T(8,128)(2,1)S(1)} %get-tuple-element.134), channel_id=1, source_target_pairs={{0,1},{1,2},{2,3},{3,4},{4,5},{5,6},{6,7},{7,8},{8,9},{9,10},{10,1... | collective-permute-start | bytes 983048 | tf_op jit(solution)/shard_map/ppermute | solution.py:25
  123.3 45.8 %collective-permute-start.19 = (bf16[320,512]{1,0:T(8,128)(2,1)S(1)}, bf16[320,512]{1,0:T(8,128)(2,1)S(1)}, u32[]{:S(2)}, u32[]{:S(2)}) collective-permute-start(bf16[320,512]{1,0:T(8,128)(2,1)S(1)} %get-tuple-element.134), channel_id=1, source_target_pairs={{1,0},{2,1},{3,2},{4,3},{5,4},{6,5},{7,6},{8,7},{9,8},{10,9},{11,1... | collective-permute-start | bytes 983048 | tf_op jit(solution)/shard_map/ppermute | solution.py:27
  127.8 9.9 %collective-permute-start.9 = (bf16[320,512]{1,0:T(8,128)(2,1)S(1)}, bf16[320,512]{1,0:T(8,128)(2,1)S(1)}, u32[]{:S(2)}, u32[]{:S(2)}) collective-permute-start(bf16[320,512]{1,0:T(8,128)(2,1)S(1)} %add_convert_fusion.6), channel_id=1, source_target_pairs={{16,0},{17,1},{18,2},{19,3},{20,4},{21,5},{22,6},{23,7},{24,8},{25... | collective-permute-start | bytes 983048 | tf_op jit(solution)/shard_map/ppermute | solution.py:37
  155.4 14.9 %collective-permute-start.15 = (bf16[320,512]{1,0:T(8,128)(2,1)S(1)}, bf16[320,512]{1,0:T(8,128)(2,1)S(1)}, u32[]{:S(2)}, u32[]{:S(2)}) collective-permute-start(bf16[320,512]{1,0:T(8,128)(2,1)S(1)} %get-tuple-element.129), channel_id=1, source_target_pairs={{0,1},{1,2},{2,3},{3,4},{4,5},{5,6},{6,7},{7,8},{8,9},{9,10},{10,1... | collective-permute-start | bytes 983048 | tf_op jit(solution)/shard_map/ppermute | solution.py:25
  164.3 9.1 %collective-permute-start.16 = (bf16[320,512]{1,0:T(8,128)(2,1)S(1)}, bf16[320,512]{1,0:T(8,128)(2,1)S(1)}, u32[]{:S(2)}, u32[]{:S(2)}) collective-permute-start(bf16[320,512]{1,0:T(8,128)(2,1)S(1)} %get-tuple-element.130), channel_id=1, source_target_pairs={{1,0},{2,1},{3,2},{4,3},{5,4},{6,5},{7,6},{8,7},{9,8},{10,9},{11,1... | collective-permute-start | bytes 983048 | tf_op jit(solution)/shard_map/ppermute | solution.py:27
  174.4 10.1 %copy-start.32 = (f32[320,2048]{1,0:T(8,128)S(1)}, f32[320,2048]{1,0:T(8,128)}, u32[]{:S(2)}) copy-start(f32[320,2048]{1,0:T(8,128)} %copy-done.31) | copy-start | bytes 7864324
  175.4 9.1 %collective-permute-start.17 = (bf16[320,512]{1,0:T(8,128)(2,1)S(1)}, bf16[320,512]{1,0:T(8,128)(2,1)S(1)}, u32[]{:S(2)}, u32[]{:S(2)}) collective-permute-start(bf16[320,512]{1,0:T(8,128)(2,1)S(1)} %get-tuple-element.126), channel_id=1, source_target_pairs={{16,0},{17,1},{18,2},{19,3},{20,4},{21,5},{22,6},{23,7},{24,8},{25... | collective-permute-start | bytes 983048 | tf_op jit(solution)/shard_map/ppermute | solution.py:37
  177.5 8.5 %copy-start.19 = (f32[512]{0:T(512)S(1)}, f32[512]{0:T(512)}, u32[]{:S(2)}) copy-start(f32[512]{0:T(512)} %get-tuple-element.140) | copy-start | bytes 6148
  184.5 30.0 %copy-start.12 = (bf16[320,512]{1,0:T(8,128)(2,1)}, bf16[320,512]{1,0:T(8,128)(2,1)S(1)}, u32[]{:S(2)}) copy-start(bf16[320,512]{1,0:T(8,128)(2,1)S(1)} %collective-permute-done.17) | copy-start | bytes 983044
  190.7 20.0 %copy-start.27 = (bf16[320,128]{1,0:T(8,128)(2,1)}, bf16[320,128]{1,0:T(8,128)(2,1)S(1)}, u32[]{:S(2)}) copy-start(bf16[320,128]{1,0:T(8,128)(2,1)S(1)} %convolution_convert_fusion.42) | copy-start | bytes 245764
  193.8 16.9 %copy-start.28 = (bf16[320,128]{1,0:T(8,128)(2,1)}, bf16[320,128]{1,0:T(8,128)(2,1)S(1)}, u32[]{:S(2)}) copy-start(bf16[320,128]{1,0:T(8,128)(2,1)S(1)} %convolution_convert_fusion.41) | copy-start | bytes 245764
  195.1 15.6 %copy-start.29 = (bf16[320,128]{1,0:T(8,128)(2,1)}, bf16[320,128]{1,0:T(8,128)(2,1)S(1)}, u32[]{:S(2)}) copy-start(bf16[320,128]{1,0:T(8,128)(2,1)S(1)} %convolution_convert_fusion.40) | copy-start | bytes 245764
  196.4 14.3 %copy-start.30 = (bf16[320,128]{1,0:T(8,128)(2,1)}, bf16[320,128]{1,0:T(8,128)(2,1)S(1)}, u32[]{:S(2)}) copy-start(bf16[320,128]{1,0:T(8,128)(2,1)S(1)} %convolution_convert_fusion.39) | copy-start | bytes 245764
  203.5 17.3 %collective-permute-start.20 = (bf16[320,512]{1,0:T(8,128)(2,1)}, bf16[320,512]{1,0:T(8,128)(2,1)}, u32[]{:S(2)}, u32[]{:S(2)}) collective-permute-start(bf16[320,512]{1,0:T(8,128)(2,1)} %get-tuple-element.127), channel_id=1, source_target_pairs={{0,1},{1,2},{2,3},{3,4},{4,5},{5,6},{6,7},{7,8},{8,9},{9,10},{10,1... | collective-permute-start | bytes 983048 | tf_op jit(solution)/shard_map/ppermute | solution.py:25
  203.5 17.3 %collective-permute-start.21 = (bf16[320,512]{1,0:T(8,128)(2,1)}, bf16[320,512]{1,0:T(8,128)(2,1)}, u32[]{:S(2)}, u32[]{:S(2)}) collective-permute-start(bf16[320,512]{1,0:T(8,128)(2,1)} %get-tuple-element.128), channel_id=1, source_target_pairs={{1,0},{2,1},{3,2},{4,3},{5,4},{6,5},{7,6},{8,7},{9,8},{10,9},{11,1... | collective-permute-start | bytes 983048 | tf_op jit(solution)/shard_map/ppermute | solution.py:27
  212.5 2.8 copy-start.35
  223.9 62.7 %copy-start.26 = (f32[1,512]{1,0:T(1,128)S(1)}, f32[1,512]{1,0:T(1,128)}, u32[]{:S(2)}) copy-start(f32[1,512]{1,0:T(1,128)} %param.25) | copy-start | bytes 6148
  286.6 2.8 copy-start.8
  360.8 4.3 %copy-start.9 = (bf16[1,2048,512]{2,1,0:T(8,128)(2,1)S(1)}, bf16[1,2048,512]{2,1,0:T(8,128)(2,1)}, u32[]{:S(2)}) copy-start(bf16[1,2048,512]{2,1,0:T(8,128)(2,1)} %get-tuple-element.101) | copy-start | bytes 6291460
  365.1 2.6 copy-start.10
  367.7 2.1 copy-start.11
  (11 other events, 13.3 us)
Sparse Core Ops, SparseCore 0:
  220.3 140.4 all-reduce.3
